TPU v7x, 256 devices: a whole 4x4x8 slice. The times are simulated.
256 devices in a mesh: chan: 32 (over y_hi, z, core), hour: 8 (over y_lo, x).
Axes of the slice: x: 4, y: 4 (y_hi: 2, y_lo: 2; y = y_hi * 2 + y_lo), z: 8, core: 2. Of those that a mesh axis runs over, the one named last changes fastest.
Arguments:
- spectra: float32 [48, 256, 2, 4096], P('hour', 'chan'), may hold values from -2.5 to 2.5
- smooth_kernel: bfloat16 [3, 32, 128, 128], P(None, 'hour'), may hold values from -0.3125 to 0.3125
- owner_ids: int32 [4], replicated, may hold values from 0 to 31, as said below
- turn_order: int32 [4], replicated, may hold values from 0 to 3, each once
- source_pick: int32 [1024], P('chan'), may hold values from 0 to 7
- receiver_pick: int32 [1024], P('chan'), may hold values from 0 to 7
Outputs:
- correlations: bfloat16 [4, 1024, 2, 4096], P(None, 'chan', None, 'hour')
Inputs may be any that keep to these rules, and one draw needn't show every extreme that they name: `owner_ids`: distinct indices along chan.
All inputs are finite; a program needn't handle non-finite values.
Results may differ from a plain program's by a relative error of at most 0.0049.
Values may be sent and summed in bfloat16 or wider, within the bound.
A program may use at most 128 MiB of HBM per device.

v0:
```python
import jax
import jax.numpy as jnp
from jax import lax
from jax.sharding import PartitionSpec as P

BAND = 128
TURNS = 4


def from_root(value, axis, source):
    kept = jnp.where(lax.axis_index(axis) == source, value, 0).astype(value.dtype)
    return lax.psum(kept, axis)


def extended(block, sides, width):
    for axis, dim in sides:
        count = lax.axis_size(axis)
        forward = [(i, i + 1) for i in range(count - 1)]
        backward = [(target, source) for source, target in forward]
        low = lax.ppermute(
            lax.slice_in_dim(block, block.shape[dim] - width, None, axis=dim), axis, forward
        )
        high = lax.ppermute(lax.slice_in_dim(block, 0, width, axis=dim), axis, backward)
        block = jnp.concatenate([low, block, high], axis=dim)
    return block


def correlate(source_block, receiver_block, source_index, receiver_index):
    source_rows = jnp.take(source_block, source_index, axis=1)
    receiver_rows = jnp.take(receiver_block, receiver_index, axis=1)
    source_real = source_rows[:, :, 0]
    source_imag = source_rows[:, :, 1]
    receiver_real = receiver_rows[:, :, 0]
    receiver_imag = receiver_rows[:, :, 1]
    real_part = jnp.sum(source_real * receiver_real + source_imag * receiver_imag, axis=0)
    imag_part = jnp.sum(source_imag * receiver_real - source_real * receiver_imag, axis=0)
    return jnp.stack([real_part, imag_part], axis=1)


def apply_kernel(padded, kernel):
    block_count = kernel.shape[1]
    block_width = kernel.shape[2]
    blocks = padded.reshape(padded.shape[:-1] + (block_count + 2, block_width))
    summed = jnp.zeros(padded.shape[:-1] + (block_count, block_width), jnp.float32)
    for offset in range(3):
        window = blocks[..., offset : offset + block_count, :]
        summed = summed + jnp.einsum(
            "...ia,iab->...ib", window, kernel[offset], preferred_element_type=jnp.float32
        )
    merged = summed.reshape(padded.shape[:-1] + (block_count * block_width,))
    return merged.astype(jnp.bfloat16)


def local(spectra, smooth_kernel, owner_ids, turn_order, source_pick, receiver_pick):
    kept_stacks = []
    for turn_index in range(TURNS):
        owner_index = owner_ids[turn_order[turn_index]]
        source = from_root(spectra, "chan", owner_index)
        partial_value = correlate(source, spectra, source_pick, receiver_pick)
        stacked = lax.psum_scatter(partial_value, "hour", scatter_dimension=2, tiled=True)
        stacked = stacked.astype(jnp.bfloat16)
        kept_stacks.append(stacked)
    gathered_stacks = jnp.stack(kept_stacks, axis=0)
    padded_all = extended(gathered_stacks, (("hour", 3),), BAND)
    result = apply_kernel(padded_all, smooth_kernel)
    return result


def solution(mesh):
    return jax.shard_map(
        local,
        mesh=mesh,
        in_specs=(
            P("hour", "chan", None, None),
            P(None, "hour", None, None),
            P(),
            P(),
            P("chan"),
            P("chan"),
        ),
        out_specs=P(None, "chan", None, "hour"),
        check_vma=False,
    )
```

profile of v0, /device:TPU:2, one launch (start us, length us, event | category | flops | bytes accessed | tf_op | source)
XLA Modules:
  0.0 640.2 jit_solution(12563146293507667906)
XLA Ops:
  6.5 1.4 fusion.14
  15.6 1.5 fusion.13
  19.6 6.8 %broadcast_select_fusion.2 = (f32[6,8,2,4096]{3,2,1,0:T(2,128)}, f32[6,8,2,4096]{3,2,1,0:T(2,128)}, f32[6,8,2,4096]{3,2,1,0:T(2,128)}, f32[6,8,2,4096]{3,2,1,0:T(2,128)}) fusion(f32[6,8,2,4096]{3,2,1,0:T(2,128)} %param.8, pred[]{:T(512)S(6)} %eq.13, pred[]{:T(512)S(6)} %eq.12, pred[]{:T(512)S(6)} %eq.15, pred[]{:T(512)S(6)} %eq.14), kind=kLoop, calls=%fused_computation.20 | loop fusion | flops 1572864 | bytes 7864324 | tf_op jit(solution)/shard_map/jit(_where)/select_n | solution.py:11
  26.3 0.0 all-reduce.3.cloned.1.call-update
  26.4 0.0 reduce-scatter.5.cloned.1.call-start
  26.4 0.6 copy-done.6
  27.0 0.8 copy-done
  27.8 10.6 %gather_fusion.1 = f32[32,6,2,4096]{3,2,1,0:T(2,128)} fusion(f32[6,8,2,4096]{3,2,1,0:T(2,128)S(1)} %copy-done, s32[1024]{0:T(1024)S(1)} %pad_clamp_fusion), kind=kCustom, calls=%fused_computation.1.clone | custom fusion | bytes 12583040 | tf_op jit(solution)/shard_map/jit(_take)/gather | solution.py:30
  38.5 11.9 %select_bitcast_fusion.3 = f32[6,32,2,4096]{3,2,0,1:T(2,128)} fusion(f32[32,6,2,4096]{3,2,1,0:T(2,128)} %gather_fusion.1, pred[32]{0:T(512)(128)(4,1)S(1)} %compare_and_fusion), kind=kLoop, calls=%fused_computation.8 | loop fusion | flops 1572864 | bytes 12582944 | tf_op jit(solution)/shard_map/jit(_take)/select_n | solution.py:30
  50.4 264.5 %all-reduce.3.cloned.1.call-done = (f32[6,8,2,4096]{3,2,1,0:T(2,128)}, f32[6,8,2,4096]{3,2,1,0:T(2,128)}, f32[6,8,2,4096]{3,2,1,0:T(2,128)}, f32[6,8,2,4096]{3,2,1,0:T(2,128)}) async-done(((f32[6,8,2,4096]{3,2,1,0:T(2,128)}, f32[6,8,2,4096]{3,2,1,0:T(2,128)}, f32[6,8,2,4096]{3,2,1,0:T(2,128)}, f32[6,8,2,4096]{3,2,1,0:T(2,128)}), (f32[6,8,2,4096]{3,2,1,0:T(2,128)}, f32[6,8,2,4096]{3,2,1,0:T(2,128)}, ...) | async-done | bytes 6291472 | tf_op jit(solution)/shard_map/psum | solution.py:12
  314.9 12.0 %gather_fusion.3 = f32[32,6,2,4096]{3,2,1,0:T(2,128)} fusion(f32[6,8,2,4096]{3,2,1,0:T(2,128)} %get-tuple-element.18, s32[1024]{0:T(1024)S(1)} %pad_clamp_fusion.1), kind=kCustom, calls=%fused_computation.3.clone | custom fusion | bytes 12583040 | tf_op jit(solution)/shard_map/jit(_take)/gather | solution.py:29
  326.9 0.0 copy-done.3
  326.9 10.6 %gather_fusion.4 = f32[32,6,2,4096]{3,2,1,0:T(2,128)} fusion(f32[6,8,2,4096]{3,2,1,0:T(2,128)S(1)} %copy-done.3, s32[1024]{0:T(1024)S(1)} %pad_clamp_fusion.1), kind=kCustom, calls=%fused_computation.4.clone | custom fusion | bytes 12583040 | tf_op jit(solution)/shard_map/jit(_take)/gather | solution.py:29
  337.6 0.0 copy-done.2
  337.6 10.5 %gather_fusion = f32[32,6,2,4096]{3,2,1,0:T(2,128)} fusion(f32[6,8,2,4096]{3,2,1,0:T(2,128)S(1)} %copy-done.2, s32[1024]{0:T(1024)S(1)} %pad_clamp_fusion.1), kind=kCustom, calls=%fused_computation.clone | custom fusion | bytes 12583040 | tf_op jit(solution)/shard_map/jit(_take)/gather | solution.py:29
  348.1 10.5 %gather_fusion.2 = f32[32,6,2,4096]{3,2,1,0:T(2,128)} fusion(f32[6,8,2,4096]{3,2,1,0:T(2,128)S(1)} %copy-done.1, s32[1024]{0:T(1024)S(1)} %pad_clamp_fusion.1), kind=kCustom, calls=%fused_computation.2.clone | custom fusion | bytes 12583040 | tf_op jit(solution)/shard_map/jit(_take)/gather | solution.py:29
  358.6 28.4 %select_bitcast_fusion.2 = (f32[6,32,2,4096]{3,2,0,1:T(2,128)}, f32[6,32,2,4096]{3,2,0,1:T(2,128)}, f32[6,32,2,4096]{3,2,0,1:T(2,128)}, f32[6,32,2,4096]{3,2,0,1:T(2,128)}) fusion(f32[32,6,2,4096]{3,2,1,0:T(2,128)} %gather_fusion.2, pred[32]{0:T(512)(128)(4,1)S(1)} %compare_and_fusion.1, f32[32,6,2,4096]{3,2,1,0:T(2,128)} %gather_fusion.3, ...), kind=kLoop, calls=%fused_computation.7 | loop fusion | flops 6291456 | bytes 50331680 | tf_op jit(solution)/shard_map/jit(_take)/select_n | solution.py:29
  386.9 65.8 %add_reduce_fusion.3 = (f32[32,4096]{1,0:T(8,128)S(1)}, f32[32,4096]{1,0:T(8,128)S(1)}, f32[32,4096]{1,0:T(8,128)S(1)}, f32[32,4096]{1,0:T(8,128)S(1)}, f32[32,4...) fusion(f32[6,32,2,4096]{3,2,0,1:T(2,128)} %get-tuple-element.38, ...), kind=kLoop, calls=%fused_computation.17 | loop fusion | flops 24117248 | bytes 35651584 | tf_op jit(solution)/shard_map/reduce_sum | solution.py:35
  452.7 1.1 pad_maximum_fusion
  453.8 0.0 reduce-scatter.5.cloned.1.call-update
  453.8 0.0 reduce-scatter.7.cloned.1.call-start
  453.9 1.1 pad_maximum_fusion.1
  454.9 0.0 reduce-scatter.7.cloned.1.call-update
  454.9 0.0 reduce-scatter.11.cloned.1.call-start
  455.0 1.1 pad_maximum_fusion.3
  456.1 0.0 reduce-scatter.11.cloned.1.call-update
  456.1 0.0 reduce-scatter.9.cloned.1.call-start
  456.1 1.1 pad_maximum_fusion.2
  457.2 0.0 reduce-scatter.9.cloned.1.call-update
  457.3 34.2 %reduce-scatter.5.cloned.1.call-done = f32[32,2,512]{2,0,1:T(8,128)} async-done(((f32[32,2,4096]{2,0,1:T(8,128)}), f32[32,2,512]{2,0,1:T(8,128)}) %reduce-scatter.5.cloned.1.call-update) | async-done | bytes 131088 | tf_op jit(solution)/shard_map/reduce_scatter | solution.py:60
  491.4 0.9 convert_bitcast_fusion.3
  492.3 42.1 %reduce-scatter.7.cloned.1.call-done = f32[32,2,512]{2,0,1:T(8,128)} async-done(((f32[32,2,4096]{2,0,1:T(8,128)}), f32[32,2,512]{2,0,1:T(8,128)}) %reduce-scatter.7.cloned.1.call-update) | async-done | bytes 131088 | tf_op jit(solution)/shard_map/reduce_scatter | solution.py:60
  534.5 0.9 convert_bitcast_fusion.2
  535.4 41.9 %reduce-scatter.11.cloned.1.call-done = f32[32,2,512]{2,0,1:T(8,128)} async-done(((f32[32,2,4096]{2,0,1:T(8,128)}), f32[32,2,512]{2,0,1:T(8,128)}) %reduce-scatter.11.cloned.1.call-update) | async-done | bytes 131088 | tf_op jit(solution)/shard_map/reduce_scatter | solution.py:60
  577.3 0.9 convert_bitcast_fusion
  578.2 41.9 %reduce-scatter.9.cloned.1.call-done = f32[32,2,512]{2,0,1:T(8,128)} async-done(((f32[32,2,4096]{2,0,1:T(8,128)}), f32[32,2,512]{2,0,1:T(8,128)}) %reduce-scatter.9.cloned.1.call-update) | async-done | bytes 131088 | tf_op jit(solution)/shard_map/reduce_scatter | solution.py:60
  620.1 0.9 convert_bitcast_fusion.1
  621.1 3.8 collective-permute-start
  624.9 2.6 collective-permute-start.1
  627.5 0.3 collective-permute-done
  627.8 3.2 collective-permute-done.1
  631.1 0.5 reshape.34
  631.6 0.4 fusion.12
  632.0 0.2 fusion.4
  632.2 0.2 convolution_add_fusion.1
  632.4 0.2 fusion.1
  632.6 0.2 copy.15
  632.8 0.8 reshape.93
  (19 shorter events, 0.1 us)
Async XLA Ops:
  6.5 308.4 %all-reduce.3.cloned.1.call-start = ((), (), s32[]{:S(2)}) async-start(), calls=%async_computation.8 | async-start | bytes 12582912 | tf_op jit(solution)/shard_map/psum | solution.py:12
  26.3 0.7 copy-start.6
  26.3 1.4 copy-start
  26.4 465.1 %reduce-scatter.5.cloned.1.call-start = ((), (), s32[]{:S(2)}) async-start(), calls=%async_computation.4 | async-start | bytes 1179648 | tf_op jit(solution)/shard_map/reduce_scatter | solution.py:60
  27.8 10.7 %copy-start.5 = (s32[32]{0:T(128)S(1)}, s32[32]{0:T(128)}, u32[]{:S(2)}) copy-start(s32[32]{0:T(128)} %param.12) | copy-start | bytes 388
  314.9 12.0 %copy-start.3 = (f32[6,8,2,4096]{3,2,1,0:T(2,128)S(1)}, f32[6,8,2,4096]{3,2,1,0:T(2,128)}, u32[]{:S(2)}) copy-start(f32[6,8,2,4096]{3,2,1,0:T(2,128)} %get-tuple-element.19) | copy-start | bytes 4718596
  326.9 10.7 %copy-start.2 = (f32[6,8,2,4096]{3,2,1,0:T(2,128)S(1)}, f32[6,8,2,4096]{3,2,1,0:T(2,128)}, u32[]{:S(2)}) copy-start(f32[6,8,2,4096]{3,2,1,0:T(2,128)} %get-tuple-element.20) | copy-start | bytes 4718596
  337.6 10.5 %copy-start.1 = (f32[6,8,2,4096]{3,2,1,0:T(2,128)S(1)}, f32[6,8,2,4096]{3,2,1,0:T(2,128)}, u32[]{:S(2)}) copy-start(f32[6,8,2,4096]{3,2,1,0:T(2,128)} %get-tuple-element.21) | copy-start | bytes 4718596
  453.8 80.7 %reduce-scatter.7.cloned.1.call-start = ((), (), s32[]{:S(2)}) async-start(), calls=%async_computation.5 | async-start | bytes 1179648 | tf_op jit(solution)/shard_map/reduce_scatter | solution.py:60
  454.9 122.3 %reduce-scatter.11.cloned.1.call-start = ((), (), s32[]{:S(2)}) async-start(), calls=%async_computation.7 | async-start | bytes 1179648 | tf_op jit(solution)/shard_map/reduce_scatter | solution.py:60
  456.1 164.0 %reduce-scatter.9.cloned.1.call-start = ((), (), s32[]{:S(2)}) async-start(), calls=%async_computation.6 | async-start | bytes 1179648 | tf_op jit(solution)/shard_map/reduce_scatter | solution.py:60
  457.2 174.7 %copy-start.4 = (bf16[3,4,128,128]{3,2,1,0:T(8,128)(2,1)S(1)}, bf16[3,4,128,128]{3,2,1,0:T(8,128)(2,1)}, u32[]{:S(2)}) copy-start(bf16[3,4,128,128]{3,2,1,0:T(8,128)(2,1)} %param.9) | copy-start | bytes 1179652
  621.1 6.8 %collective-permute-start = (bf16[4,32,2,128]{3,1,2,0:T(8,128)(2,1)S(1)}, bf16[4,32,2,128]{3,1,2,0:T(8,128)(2,1)S(1)}, u32[]{:S(2)}, u32[]{:S(2)}) collective-permute-start(bf16[4,32,2,128]{3,1,2,0:T(8,128)(2,1)S(1)} %get-tuple-element.33), channel_id=1, source_target_pairs={{0,1},{1,2},{2,3},{3,4},{4,5},{5,6},{6,7},{8,9},{9,10},{10,11},{11... | collective-permute-start | bytes 196616 | tf_op jit(solution)/shard_map/ppermute | solution.py:20
  624.9 6.2 collective-permute-start.1
Sparse Core Ops, SparseCore 0:
  26.5 288.3 all-reduce.2
  453.9 37.4 reduce-scatter.4
  494.0 40.4 reduce-scatter.6
  536.8 40.3 reduce-scatter.10
  579.7 40.3 reduce-scatter.8
where the time goes:
time: 644 us; the launch traced here: 640 us
  waiting for transfers between devices  428 us (66%)
  other arithmetic  121 us (19%)
  local copies, waits for them, and re-layouts  60.4 us (9%)
  between operations  23.4 us (4%)
  starting transfers between devices  6.61 us (1%)
    psum x1, waiting for transfers between devices, from_root(): return lax.psum(kept, axis)  265 us
    reduce_scatter x4, waiting for transfers between devices, local(): lax.psum_scatter(partial_value, 'hour', scatter_dimension=2, tiled=True)  160 us
    reduce_sum x1, other arithmetic, correlate(): jnp.sum(source_real * receiver_real + source_imag * receiver_imag, axis=0)  65.8 us
    gather x4, local copies, waits for them, and re-layouts, correlate(): source_rows = jnp.take(source_block, source_index, axis=1)  43.6 us
    select_n x2, other arithmetic, correlate(): source_rows = jnp.take(source_block, source_index, axis=1)  28.4 us
  transfers between devices with their start and end apart: 7, of which 7 were waited for; matrix products, arithmetic and copies ran while one was open for 4% of the time, Pallas kernels for 0%

commit v1 on v0

v1 whole, which is shorter than its diff:
```python
import jax
import jax.numpy as jnp
from jax import lax
from jax.experimental import pallas as pl
from jax.experimental.pallas import tpu as pltpu
from jax.sharding import PartitionSpec as P

MESH = pl.DeviceIdType.MESH

BAND = 128
TURNS = 4
C_DEV = 8
PAIRS = 32
HOUR_DEVS = 8
HOURS_DEV = 6
Z = 8
GROUPS = 4
ROWS = HOURS_DEV * 16
NB = 32
BF16 = jnp.bfloat16
F32 = jnp.float32


def body(
    spectra, kernel, owner_ids, turn_order, source_pick, receiver_pick, out,
    raw, staged, recv, up, down, chosen, acc, onehot, picked, halo, merged,
    raw_sem, a2a_send, a2a_recv, up_send, up_recv, down_send, down_recv,
    hot_send, hot_recv, out_send, out_recv, edge_send, self_sem,
):
    chan = lax.axis_index("chan")
    hour = lax.axis_index("hour")
    core = chan % 2
    z = (chan // 2) % Z
    y_hi = chan // (2 * Z)
    group = y_hi * 2 + core

    def chan_of(g, level):
        return ((g // 2) * Z + level) * 2 + g % 2

    load = pltpu.make_async_copy(spectra, raw, raw_sem)
    load.start()

    barrier = pltpu.get_barrier_semaphore()

    def greet(n, _):
        g, h = n // HOUR_DEVS, n % HOUR_DEVS

        @pl.when(jnp.logical_or(g != group, h != hour))
        def _():
            pl.semaphore_signal(
                barrier, inc=1, device_id=(chan_of(g, z), h), device_id_type=MESH
            )

        return 0

    above = chan_of(group, (z + 1) % Z)
    below = chan_of(group, (z + Z - 1) % Z)
    lax.fori_loop(0, NB, greet, 0)
    pl.semaphore_signal(barrier, inc=1, device_id=(above, hour), device_id_type=MESH)
    pl.semaphore_signal(barrier, inc=1, device_id=(below, hour), device_id_type=MESH)

    src = source_pick[...]
    rec = receiver_pick[...]
    code = (((rec - src) & 7) * 16 + src).astype(F32)
    row = lax.broadcasted_iota(jnp.int32, (PAIRS, PAIRS), 0)
    col = lax.broadcasted_iota(jnp.int32, (PAIRS, PAIRS), 1)
    spread = jnp.where(row == col, jnp.broadcast_to(code, (PAIRS, PAIRS)), 0.0)
    code_col = jnp.sum(spread, axis=1, keepdims=True)
    lane = lax.broadcasted_iota(jnp.int32, (PAIRS, BAND), 1).astype(F32)
    for c in range(2):
        hot = jnp.where(lane == code_col + 8.0 * c, 1.0, 0.0)
        onehot[group, pl.ds(c * PAIRS, PAIRS), :] = hot.astype(BF16)

    acc[...] = jnp.zeros_like(acc)

    @pl.when(hour == 0)
    def _():
        halo[0] = jnp.zeros((2 * TURNS * PAIRS, BAND), BF16)

    @pl.when(hour == HOUR_DEVS - 1)
    def _():
        halo[5] = jnp.zeros((2 * TURNS * PAIRS, BAND), BF16)

    load.wait()
    pl.semaphore_wait(barrier, NB + 1)

    def a2a(g, h):
        band = h * GROUPS + g
        return pltpu.make_async_remote_copy(
            src_ref=staged.at[band],
            dst_ref=recv.at[group, hour],
            send_sem=a2a_send.at[band],
            recv_sem=a2a_recv.at[group, hour],
            device_id=(chan_of(g, z), h),
            device_id_type=MESH,
        )

    def scatter(n, _):
        k = n // GROUPS
        g = (group + n) % GROUPS
        step = (k + 1) // 2
        shift = jnp.where(k % 2 == 1, step, 2 * Z - step)
        h = (hour + 4 * Z - z - shift) % HOUR_DEVS
        band = h * GROUPS + g
        mine = jnp.logical_and(g == group, h == hour)
        for i in range(HOURS_DEV):
            parts = [
                raw[pl.ds(i * 512 + band * 2 + p, 8, stride=64), :] for p in range(2)
            ]
            staged[band, pl.ds(i * 16, 16), :] = jnp.concatenate(parts, 0).astype(BF16)

        @pl.when(jnp.logical_not(mine))
        def _():
            a2a(g, h).start()

        @pl.when(mine)
        def _():
            recv[group, hour] = staged[band]

        return 0

    lax.fori_loop(0, NB, scatter, 0)

    def hot_copy(g):
        return pltpu.make_async_remote_copy(
            src_ref=onehot.at[group],
            dst_ref=onehot.at[group],
            send_sem=hot_send.at[g],
            recv_sem=hot_recv.at[group],
            device_id=(chan_of(g, z), hour),
            device_id_type=MESH,
        )

    def hot_wait(g):
        return pltpu.make_async_remote_copy(
            src_ref=onehot.at[group],
            dst_ref=onehot.at[g],
            send_sem=hot_send.at[g],
            recv_sem=hot_recv.at[g],
            device_id=(chan_of(g, z), hour),
            device_id_type=MESH,
        )

    def others(fn):
        def each(n, _):
            fn((group + n) % GROUPS)
            return 0

        lax.fori_loop(1, GROUPS, each, 0)

    others(lambda g: hot_copy(g).start())

    owners = [owner_ids[turn_order[t]] for t in range(TURNS)]
    owner_z = [(o // 2) % Z for o in owners]
    owner_g = [(o // (2 * Z)) * 2 + o % 2 for o in owners]

    def wait_pieces(h):
        def each(g, _):
            @pl.when(jnp.logical_or(g != group, h != hour))
            def _():
                pltpu.make_async_remote_copy(
                    src_ref=staged.at[0],
                    dst_ref=recv.at[g, h],
                    send_sem=a2a_send.at[0],
                    recv_sem=a2a_recv.at[g, h],
                    device_id=(chan_of(g, z), h),
                    device_id_type=MESH,
                ).wait_recv()

            return 0

        lax.fori_loop(0, GROUPS, each, 0)

    def merge(buf, s, h, first):
        for i in range(HOURS_DEV):
            rows = pl.ds(i * 16, 16)
            held = [recv[g, h, rows, :].astype(F32) for g in range(GROUPS)]
            for t in range(TURNS):
                mine = held[0]
                for g in range(1, GROUPS):
                    mine = lax.select_n(owner_g[t] == g, mine, held[g])
                if not first:
                    mine = lax.select_n(
                        owner_z[t] == z, buf[s, t, rows, :].astype(F32), mine
                    )
                buf[s, t, rows, :] = mine.astype(BF16)

    def hop(buf, s, send, arrive, target):
        return pltpu.make_async_remote_copy(
            src_ref=buf.at[s],
            dst_ref=buf.at[s + 1],
            send_sem=send.at[s],
            recv_sem=arrive.at[s + 1],
            device_id=(target, hour),
            device_id_type=MESH,
        )

    def arrived(buf, s, send, arrive, source):
        pltpu.make_async_remote_copy(
            src_ref=buf.at[0],
            dst_ref=buf.at[s],
            send_sem=send.at[0],
            recv_sem=arrive.at[s],
            device_id=(source, hour),
            device_id_type=MESH,
        ).wait_recv()

    def hour_of(q):
        return (q + hour + 4 * Z) % HOUR_DEVS

    def choose(r, slot):
        q = z - r + 2 * Z
        for t in range(TURNS):
            position = (owner_z[t] + 4 * Z - q) % Z
            lower = position < jnp.maximum(r, 1)
            for i in range(HOURS_DEV):
                rows = pl.ds(i * 16, 16)
                value = lax.select_n(
                    lower,
                    down[Z - 1 - r, t, rows, :].astype(F32),
                    up[r, t, rows, :].astype(F32),
                )
                chosen[t, slot, rows, :] = value

    def multiply(g, t0, hours):
        start = tuple(
            acc[g, t0 + t, k, c] for t in range(2) for k in range(8) for c in range(2)
        )

        def each(n, sums):
            slot, i = n // HOURS_DEV, n % HOURS_DEV
            h = jnp.where(slot == 0, hours[0], hours[1])
            rows = pl.ds(pl.multiple_of(i * 16, 16), 16)
            b = recv[g, h, rows, :].astype(F32)
            b0, b1 = b[:8], b[8:]
            a = [chosen[t0 + t, slot, rows, :] for t in range(2)]
            new = list(sums)
            for k in range(8):
                r0 = pltpu.roll(b0, 8 - k, 0) if k else b0
                r1 = pltpu.roll(b1, 8 - k, 0) if k else b1
                for t in range(2):
                    a0, a1 = a[t][:8], a[t][8:]
                    at = (t * 8 + k) * 2
                    new[at] = new[at] + (a0 * r0 + a1 * r1)
                    new[at + 1] = new[at + 1] + (a1 * r0 - a0 * r1)
            return tuple(new)

        sums = lax.fori_loop(0, 2 * HOURS_DEV, each, start)
        n = 0
        for t in range(2):
            for k in range(8):
                for c in range(2):
                    acc[g, t0 + t, k, c] = sums[n]
                    n += 1

    def step(s, first, send):
        low, high = hour_of(z - s), hour_of(z + 1 + s)
        if not first:
            arrived(up, s, up_send, up_recv, below)
        if send:
            merge(up, s, low, first)
            hop(up, s, up_send, up_recv, above).start()
        if not first:
            arrived(down, s, down_send, down_recv, above)
        if send:
            merge(down, s, high, first)
            hop(down, s, down_send, down_recv, below).start()
        return low, high

    def early(s, _):
        wait_pieces(hour_of(z - s))
        wait_pieces(hour_of(z + 1 + s))
        step(s, False, True)
        return 0

    def late(s, _):
        low, high = step(s, False, True)
        choose(s, 0)
        choose(Z - 1 - s, 1)

        def each(n, _):
            multiply(n // 2, (n % 2) * 2, (low, high))
            return 0

        lax.fori_loop(0, GROUPS * 2, each, 0)
        return 0

    wait_pieces(hour_of(z))
    wait_pieces(hour_of(z + 1))
    step(0, True, True)
    lax.fori_loop(1, 4, early, 0)
    lax.fori_loop(4, Z - 1, late, 0)
    low, high = step(Z - 1, False, False)
    choose(Z - 1, 0)
    choose(0, 1)
    others(lambda g: hot_wait(g).wait_recv())

    def deliver(g):
        return pltpu.make_async_remote_copy(
            src_ref=picked.at[g],
            dst_ref=halo.at[1 + group],
            send_sem=out_send.at[g],
            recv_sem=out_recv.at[1 + group],
            device_id=(chan_of(g, z), hour),
            device_id_type=MESH,
        )

    def edge(g, to, slot):
        return pltpu.make_async_remote_copy(
            src_ref=picked.at[g],
            dst_ref=halo.at[slot],
            send_sem=edge_send.at[g],
            recv_sem=out_recv.at[slot],
            device_id=(chan_of(g, z), to),
            device_id_type=MESH,
        )

    to_low = jnp.logical_and(group == 0, hour > 0)
    to_high = jnp.logical_and(group == GROUPS - 1, hour < HOUR_DEVS - 1)

    def finish(n, _):
        g = (group + 1 + n) % GROUPS
        multiply(g, 0, (low, high))
        multiply(g, 2, (low, high))
        for t in range(TURNS):
            table = jnp.concatenate(
                [acc[g, t, k, c] for k in range(8) for c in range(2)], axis=0
            ).astype(BF16)
            rows = jnp.dot(onehot[g], table, preferred_element_type=F32)
            picked[g, pl.ds(t * 2 * PAIRS, 2 * PAIRS), :] = rows.astype(BF16)

        @pl.when(g != group)
        def _():
            deliver(g).start()

        @pl.when(g == group)
        def _():
            halo[1 + group] = picked[g]

        @pl.when(to_low)
        def _():
            edge(g, hour - 1, 5).start()

        @pl.when(to_high)
        def _():
            edge(g, hour + 1, 0).start()

        return 0

    lax.fori_loop(0, GROUPS, finish, 0)

    def out_wait(slot):
        pltpu.make_async_remote_copy(
            src_ref=picked.at[0],
            dst_ref=halo.at[slot],
            send_sem=out_send.at[0],
            recv_sem=out_recv.at[slot],
            device_id=(chan, hour),
            device_id_type=MESH,
        ).wait_recv()

    others(lambda g: out_wait(1 + g))

    @pl.when(hour > 0)
    def _():
        out_wait(0)

    @pl.when(hour < HOUR_DEVS - 1)
    def _():
        out_wait(5)

    for b in range(4):
        total = jnp.dot(halo[b], kernel[0, b], preferred_element_type=F32)
        for d in range(1, 3):
            total += jnp.dot(halo[b + d], kernel[d, b], preferred_element_type=F32)
        for t in range(TURNS):
            for c in range(2):
                for p in range(0, PAIRS, 8):
                    at = t * 2 * PAIRS + c * PAIRS + p
                    merged[pl.ds((t * PAIRS + p) * 8 + b * 2 + c, 8, stride=8), :] = (
                        total[at : at + 8]
                    )
    out[...] = merged[...].astype(BF16)

    def drain(n, _):
        g, h = n // HOUR_DEVS, n % HOUR_DEVS

        @pl.when(jnp.logical_or(g != group, h != hour))
        def _():
            a2a(g, h).wait_send()

        return 0

    lax.fori_loop(0, NB, drain, 0)
    others(lambda g: hot_copy(g).wait_send())
    others(lambda g: deliver(g).wait_send())

    def drain_hops(s, _):
        hop(up, s, up_send, up_recv, above).wait_send()
        hop(down, s, down_send, down_recv, below).wait_send()
        return 0

    lax.fori_loop(0, Z - 1, drain_hops, 0)

    @pl.when(jnp.logical_or(to_low, to_high))
    def _():
        def each(g, _):
            edge(g, hour, 0).wait_send()
            return 0

        lax.fori_loop(0, GROUPS, each, 0)


def local(spectra, smooth_kernel, owner_ids, turn_order, source_pick, receiver_pick):
    tiles = spectra.reshape(HOURS_DEV, C_DEV, 2, NB, BAND)
    tiles = tiles.transpose(0, 1, 3, 2, 4).reshape(HOURS_DEV * C_DEV * NB * 2, BAND)
    vmem = pl.BlockSpec(memory_space=pltpu.VMEM)
    smem = pl.BlockSpec(memory_space=pltpu.SMEM)
    rows = TURNS * 2 * PAIRS
    dma = pltpu.SemaphoreType.DMA
    result = pl.pallas_call(
        body,
        out_shape=jax.ShapeDtypeStruct((rows * 4, BAND), BF16),
        in_specs=[pl.BlockSpec(memory_space=pl.ANY), vmem, smem, smem, vmem, vmem],
        out_specs=vmem,
        scratch_shapes=[
            pltpu.VMEM((HOURS_DEV * C_DEV * NB * 2, BAND), F32),
            pltpu.VMEM((NB, ROWS, BAND), BF16),
            pltpu.VMEM((GROUPS, HOUR_DEVS, ROWS, BAND), BF16),
            pltpu.VMEM((Z, TURNS, ROWS, BAND), BF16),
            pltpu.VMEM((Z, TURNS, ROWS, BAND), BF16),
            pltpu.VMEM((TURNS, 2, ROWS, BAND), F32),
            pltpu.VMEM((GROUPS, TURNS, 8, 2, 8, BAND), F32),
            pltpu.VMEM((GROUPS, 2 * PAIRS, BAND), BF16),
            pltpu.VMEM((GROUPS, rows, BAND), BF16),
            pltpu.VMEM((6, rows, BAND), BF16),
            pltpu.VMEM((rows * 4, BAND), F32),
            dma,
            dma((NB,)),
            dma((GROUPS, HOUR_DEVS)),
            dma((Z,)),
            dma((Z,)),
            dma((Z,)),
            dma((Z,)),
            dma((GROUPS,)),
            dma((GROUPS,)),
            dma((GROUPS,)),
            dma((6,)),
            dma((GROUPS,)),
            dma,
        ],
        compiler_params=pltpu.CompilerParams(
            collective_id=0, has_side_effects=True, vmem_limit_bytes=48 * 1024 * 1024
        ),
    )(
        tiles,
        smooth_kernel,
        owner_ids,
        turn_order,
        source_pick.reshape(1, PAIRS),
        receiver_pick.reshape(1, PAIRS),
    )
    result = result.reshape(TURNS, PAIRS, 4, 2, BAND).transpose(0, 1, 3, 2, 4)
    return result.reshape(TURNS, PAIRS, 2, 4 * BAND)


def solution(mesh):
    return jax.shard_map(
        local,
        mesh=mesh,
        in_specs=(
            P("hour", "chan", None, None),
            P(None, "hour", None, None),
            P(),
            P(),
            P("chan"),
            P("chan"),
        ),
        out_specs=P(None, "chan", None, "hour"),
        check_vma=False,
    )
```

time: 644 us -> 65.9 us (0.10)
  waiting for transfers between devices: 428 us -> 0 us
  other arithmetic: 121 us -> 0 us
  Pallas kernels: 0 us -> 60 us
  local copies, waits for them, and re-layouts: 60.4 us -> 5.73 us
  between operations: 23.4 us -> 0.02 us
  starting transfers between devices: 6.61 us -> 0 us
    psum x1 -> x0, waiting for transfers between devices: 265 us -> none  [from_root(): return lax.psum(kept, axis)]
    reduce_scatter x4 -> x0, waiting for transfers between devices: 160 us -> none  [local(): lax.psum_scatter(partial_value, 'hour', scatter_dimension=2, tiled=True)]
    reduce_sum x1 -> x0, other arithmetic: 65.8 us -> none  [correlate(): jnp.sum(source_real * receiver_real + source_imag * receiver_imag, axis=0)]
    pallas_call x0 -> x1, Pallas kernels: none -> 60 us  [local(): pl.pallas_call(body, out_shape=jax.ShapeDtypeStruct((rows * 4, BAND), BF1...]
    gather x5 -> x0, local copies, waits for them, and re-layouts: 54.3 us -> none  [the longest x4 43.6 us: correlate(): source_rows = jnp.take(source_block, source_index, axis=1)]
    select_n x5 -> x0, other arithmetic: 47.1 us -> none  [the longest x2 28.4 us: correlate(): source_rows = jnp.take(source_block, source_index, axis=1)]
    another operation x8 -> x0, other arithmetic: 7.93 us -> none  [the longest x4 4.28 us: correlate(): return jnp.stack([real_part, imag_part], axis=1)]
    ppermute x2 -> x0, starting transfers between devices: 6.45 us -> none  [the longest x1 3.83 us: extended(): lax.ppermute(lax.slice_in_dim(block, block.shape[dim] - width, None, axis...]
  transfers between devices with their start and end apart: 7 -> 0, of which waited for: 7 -> 0; matrix products, arithmetic and copies ran while one was open for 4% -> 0% of each run, Pallas kernels for 0% -> 0%
where the time goes in v1:
time: 65.9 us; the launch traced here: 65.7 us
  Pallas kernels  60 us (91%)
  local copies, waits for them, and re-layouts  5.73 us (9%)
    pallas_call x1, Pallas kernels, local(): pl.pallas_call(body, out_shape=jax.ShapeDtypeStruct((rows * 4, BAND), BF1...  60 us
    unnamed x13, local copies, waits for them, and re-layouts  5.73 us

profile of v1, /device:TPU:2, one launch (start us, length us, event | category | flops | bytes accessed | tf_op | source)
XLA Modules:
  0.0 65.7 jit_solution(13453248933206046629)
XLA Ops:
  0.0 0.0 copy-start
  0.0 1.4 %copy-done = f32[6,8,2,4096]{3,2,1,0:T(2,128)S(1)} copy-done((f32[6,8,2,4096]{3,2,1,0:T(2,128)S(1)}, f32[6,8,2,4096]{3,2,1,0:T(2,128)}, u32[]{:S(2)}) %copy-start) | copy-done | bytes 1572888
  1.4 0.0 copy-start.1
  1.4 1.0 %copy-done.1 = bf16[3,4,128,128]{3,2,1,0:T(8,128)(2,1)S(1)} copy-done((bf16[3,4,128,128]{3,2,1,0:T(8,128)(2,1)S(1)}, bf16[3,4,128,128]{3,2,1,0:T(8,128)(2,1)}, u32[]{:S(2)}) %copy-start.1) | copy-done | bytes 393240
  2.4 0.0 copy-start.2
  2.4 0.7 copy-done.2
  3.1 0.0 copy-start.3
  3.1 0.7 copy-done.3
  3.7 0.0 copy-start.4
  3.7 0.7 copy-done.4
  4.4 0.0 copy-start.5
  4.4 0.7 copy-done.5
  5.0 60.0 %shard_map.64 = bf16[1024,128]{1,0:T(8,128)(2,1)S(1)} custom-call(f32[3072,128]{1,0:T(8,128)S(1)} %bitcast.12, bf16[3,4,128,128]{3,2,1,0:T(8,128)(2,1)S(1)} %copy-done.1, s32[4]{0:T(128)S(1)} %copy-done.2, s32[4]{0:T(128)S(1)} %copy-done.3, s32[1,32]{1,0:T(1,128)S(1)} %bitcast.14, s32[1,32]{1,0:T(1,128)S(1)} %bitcast.15), custom_call_target="tpu_custom_call" | custom-call | tf_op jit(solution)/shard_map/pallas_call | solution.py:421
  65.0 0.7 %copy.10 = bf16[4,32,2,512]{3,2,1,0:T(2,128)(2,1)} copy(bf16[4,32,2,512]{3,2,1,0:T(2,128)(2,1)S(1)} %bitcast.13) | data formatting | bytes 524288
Async XLA Ops:
  0.0 1.4 %copy-start = (f32[6,8,2,4096]{3,2,1,0:T(2,128)S(1)}, f32[6,8,2,4096]{3,2,1,0:T(2,128)}, u32[]{:S(2)}) copy-start(f32[6,8,2,4096]{3,2,1,0:T(2,128)} %param.6) | copy-start | bytes 4718596
  1.4 1.0 %copy-start.1 = (bf16[3,4,128,128]{3,2,1,0:T(8,128)(2,1)S(1)}, bf16[3,4,128,128]{3,2,1,0:T(8,128)(2,1)}, u32[]{:S(2)}) copy-start(bf16[3,4,128,128]{3,2,1,0:T(8,128)(2,1)} %kernel.1) | copy-start | bytes 1179652
  2.4 0.7 copy-start.2
  3.1 0.7 copy-start.3
  3.7 0.7 copy-start.4
  4.4 0.7 copy-start.5

commit v2 on v1

--- a/solution.py
+++ b/solution.py
@@ -16,16 +16,19 @@
 Z = 8
 GROUPS = 4
 ROWS = HOURS_DEV * 16
+TG = 2
+PARTS = TURNS // TG
 NB = 32
 BF16 = jnp.bfloat16
 F32 = jnp.float32
 
 
 def body(
-    spectra, kernel, owner_ids, turn_order, source_pick, receiver_pick, out,
+    spectra, kernel_hbm, owners_hbm, order_hbm, source_pick, receiver_pick, out,
     raw, staged, recv, up, down, chosen, acc, onehot, picked, halo, merged,
-    raw_sem, a2a_send, a2a_recv, up_send, up_recv, down_send, down_recv,
-    hot_send, hot_recv, out_send, out_recv, edge_send, self_sem,
+    kernel, owner_ids, turn_order, load_sem,
+    a2a_send, a2a_recv, up_send, up_recv, down_send, down_recv,
+    hot_send, hot_recv, out_send, out_recv, edge_send,
 ):
     chan = lax.axis_index("chan")
     hour = lax.axis_index("hour")
@@ -37,8 +40,19 @@
     def chan_of(g, level):
         return ((g // 2) * Z + level) * 2 + g % 2
 
-    load = pltpu.make_async_copy(spectra, raw, raw_sem)
-    load.start()
+    loads = [
+        pltpu.make_async_copy(a, b, load_sem.at[n])
+        for n, (a, b) in enumerate(
+            [
+                (spectra, raw),
+                (owners_hbm, owner_ids),
+                (order_hbm, turn_order),
+                (kernel_hbm, kernel),
+            ]
+        )
+    ]
+    for load in loads:
+        load.start()
 
     barrier = pltpu.get_barrier_semaphore()
 
@@ -81,7 +95,8 @@
     def _():
         halo[5] = jnp.zeros((2 * TURNS * PAIRS, BAND), BF16)
 
-    load.wait()
+    for load in loads[:3]:
+        load.wait()
     pl.semaphore_wait(barrier, NB + 1)
 
     def a2a(g, h):
@@ -148,7 +163,6 @@
 
         lax.fori_loop(1, GROUPS, each, 0)
 
-    others(lambda g: hot_copy(g).start())
 
     owners = [owner_ids[turn_order[t]] for t in range(TURNS)]
     owner_z = [(o // 2) % Z for o in owners]
@@ -171,36 +185,36 @@
 
         lax.fori_loop(0, GROUPS, each, 0)
 
-    def merge(buf, s, h, first):
+    def merge(buf, s, h, t0, first):
         for i in range(HOURS_DEV):
             rows = pl.ds(i * 16, 16)
-            held = [recv[g, h, rows, :].astype(F32) for g in range(GROUPS)]
-            for t in range(TURNS):
+            held = [recv[g, h, rows, :] for g in range(GROUPS)]
+            for t in range(t0, t0 + TG):
                 mine = held[0]
                 for g in range(1, GROUPS):
                     mine = lax.select_n(owner_g[t] == g, mine, held[g])
                 if not first:
-                    mine = lax.select_n(
-                        owner_z[t] == z, buf[s, t, rows, :].astype(F32), mine
-                    )
-                buf[s, t, rows, :] = mine.astype(BF16)
-
-    def hop(buf, s, send, arrive, target):
+                    mine = lax.select_n(owner_z[t] == z, buf[s, t, rows, :], mine)
+                buf[s, t, rows, :] = mine
+
+    def hop(buf, s, part, send, arrive, target):
+        turns = pl.ds(part * TG, TG)
         return pltpu.make_async_remote_copy(
-            src_ref=buf.at[s],
-            dst_ref=buf.at[s + 1],
-            send_sem=send.at[s],
-            recv_sem=arrive.at[s + 1],
+            src_ref=buf.at[s, turns],
+            dst_ref=buf.at[s + 1, turns],
+            send_sem=send.at[s, part],
+            recv_sem=arrive.at[s + 1, part],
             device_id=(target, hour),
             device_id_type=MESH,
         )
 
-    def arrived(buf, s, send, arrive, source):
+    def arrived(buf, s, part, send, arrive, source):
+        turns = pl.ds(part * TG, TG)
         pltpu.make_async_remote_copy(
-            src_ref=buf.at[0],
-            dst_ref=buf.at[s],
-            send_sem=send.at[0],
-            recv_sem=arrive.at[s],
+            src_ref=buf.at[0, turns],
+            dst_ref=buf.at[s, turns],
+            send_sem=send.at[0, part],
+            recv_sem=arrive.at[s, part],
             device_id=(source, hour),
             device_id_type=MESH,
         ).wait_recv()
@@ -208,19 +222,17 @@
     def hour_of(q):
         return (q + hour + 4 * Z) % HOUR_DEVS
 
-    def choose(r, slot):
+    def choose(r, slot, turns):
         q = z - r + 2 * Z
-        for t in range(TURNS):
+        for t in turns:
             position = (owner_z[t] + 4 * Z - q) % Z
             lower = position < jnp.maximum(r, 1)
             for i in range(HOURS_DEV):
                 rows = pl.ds(i * 16, 16)
                 value = lax.select_n(
-                    lower,
-                    down[Z - 1 - r, t, rows, :].astype(F32),
-                    up[r, t, rows, :].astype(F32),
+                    lower, down[Z - 1 - r, t, rows, :], up[r, t, rows, :]
                 )
-                chosen[t, slot, rows, :] = value
+                chosen[t, slot, rows, :] = value.astype(F32)
 
     def multiply(g, t0, hours):
         start = tuple(
@@ -229,8 +241,8 @@
 
         def each(n, sums):
             slot, i = n // HOURS_DEV, n % HOURS_DEV
-            h = jnp.where(slot == 0, hours[0], hours[1])
-            rows = pl.ds(pl.multiple_of(i * 16, 16), 16)
+            h = hours[slot]
+            rows = pl.ds(i * 16, 16)
             b = recv[g, h, rows, :].astype(F32)
             b0, b1 = b[:8], b[8:]
             a = [chosen[t0 + t, slot, rows, :] for t in range(2)]
@@ -245,7 +257,9 @@
                     new[at + 1] = new[at + 1] + (a1 * r0 - a0 * r1)
             return tuple(new)
 
-        sums = lax.fori_loop(0, 2 * HOURS_DEV, each, start)
+        sums = start
+        for n in range(2 * HOURS_DEV):
+            sums = each(n, sums)
         n = 0
         for t in range(2):
             for k in range(8):
@@ -253,30 +267,34 @@
                     acc[g, t0 + t, k, c] = sums[n]
                     n += 1
 
-    def step(s, first, send):
+    def step(s, first):
         low, high = hour_of(z - s), hour_of(z + 1 + s)
-        if not first:
-            arrived(up, s, up_send, up_recv, below)
-        if send:
-            merge(up, s, low, first)
-            hop(up, s, up_send, up_recv, above).start()
-        if not first:
-            arrived(down, s, down_send, down_recv, above)
-        if send:
-            merge(down, s, high, first)
-            hop(down, s, down_send, down_recv, below).start()
+        for part in range(PARTS):
+            if not first:
+                arrived(up, s, part, up_send, up_recv, below)
+            merge(up, s, low, part * TG, first)
+            hop(up, s, part, up_send, up_recv, above).start()
+            if not first:
+                arrived(down, s, part, down_send, down_recv, above)
+            merge(down, s, high, part * TG, first)
+            hop(down, s, part, down_send, down_recv, below).start()
         return low, high
 
     def early(s, _):
         wait_pieces(hour_of(z - s))
         wait_pieces(hour_of(z + 1 + s))
-        step(s, False, True)
+        step(s, False)
+
+        @pl.when(s == 1)
+        def _():
+            others(lambda g: hot_copy(g).start())
+
         return 0
 
     def late(s, _):
-        low, high = step(s, False, True)
-        choose(s, 0)
-        choose(Z - 1 - s, 1)
+        low, high = step(s, False)
+        choose(s, 0, range(TURNS))
+        choose(Z - 1 - s, 1, range(TURNS))
 
         def each(n, _):
             multiply(n // 2, (n % 2) * 2, (low, high))
@@ -287,30 +305,30 @@
 
     wait_pieces(hour_of(z))
     wait_pieces(hour_of(z + 1))
-    step(0, True, True)
+    step(0, True)
     lax.fori_loop(1, 4, early, 0)
     lax.fori_loop(4, Z - 1, late, 0)
-    low, high = step(Z - 1, False, False)
-    choose(Z - 1, 0)
-    choose(0, 1)
+    low, high = hour_of(z + 1), hour_of(z)
     others(lambda g: hot_wait(g).wait_recv())
 
-    def deliver(g):
+    def deliver(g, part):
+        rows = pl.ds(part * TG * 2 * PAIRS, TG * 2 * PAIRS)
         return pltpu.make_async_remote_copy(
-            src_ref=picked.at[g],
-            dst_ref=halo.at[1 + group],
-            send_sem=out_send.at[g],
-            recv_sem=out_recv.at[1 + group],
+            src_ref=picked.at[g, rows],
+            dst_ref=halo.at[1 + group, rows],
+            send_sem=out_send.at[g, part],
+            recv_sem=out_recv.at[1 + group, part],
             device_id=(chan_of(g, z), hour),
             device_id_type=MESH,
         )
 
-    def edge(g, to, slot):
+    def edge(g, part, to, slot):
+        rows = pl.ds(part * TG * 2 * PAIRS, TG * 2 * PAIRS)
         return pltpu.make_async_remote_copy(
-            src_ref=picked.at[g],
-            dst_ref=halo.at[slot],
-            send_sem=edge_send.at[g],
-            recv_sem=out_recv.at[slot],
+            src_ref=picked.at[g, rows],
+            dst_ref=halo.at[slot, rows],
+            send_sem=edge_send.at[g, part],
+            recv_sem=out_recv.at[slot, part],
             device_id=(chan_of(g, z), to),
             device_id_type=MESH,
         )
@@ -318,69 +336,85 @@
     to_low = jnp.logical_and(group == 0, hour > 0)
     to_high = jnp.logical_and(group == GROUPS - 1, hour < HOUR_DEVS - 1)
 
-    def finish(n, _):
-        g = (group + 1 + n) % GROUPS
-        multiply(g, 0, (low, high))
-        multiply(g, 2, (low, high))
-        for t in range(TURNS):
-            table = jnp.concatenate(
-                [acc[g, t, k, c] for k in range(8) for c in range(2)], axis=0
-            ).astype(BF16)
-            rows = jnp.dot(onehot[g], table, preferred_element_type=F32)
-            picked[g, pl.ds(t * 2 * PAIRS, 2 * PAIRS), :] = rows.astype(BF16)
-
-        @pl.when(g != group)
-        def _():
-            deliver(g).start()
-
-        @pl.when(g == group)
-        def _():
-            halo[1 + group] = picked[g]
-
-        @pl.when(to_low)
-        def _():
-            edge(g, hour - 1, 5).start()
-
-        @pl.when(to_high)
-        def _():
-            edge(g, hour + 1, 0).start()
-
-        return 0
-
-    lax.fori_loop(0, GROUPS, finish, 0)
-
-    def out_wait(slot):
+    for part in range(PARTS):
+        turns = range(part * TG, part * TG + TG)
+        arrived(up, Z - 1, part, up_send, up_recv, below)
+        arrived(down, Z - 1, part, down_send, down_recv, above)
+        choose(Z - 1, 0, turns)
+        choose(0, 1, turns)
+
+        def finish(n, _, part=part, turns=turns):
+            g = (group + 1 + n) % GROUPS
+            for t in turns[::2]:
+                multiply(g, t, (low, high))
+            for t in turns:
+                table = jnp.concatenate(
+                    [acc[g, t, k, c] for k in range(8) for c in range(2)], axis=0
+                ).astype(BF16)
+                rows = jnp.dot(onehot[g], table, preferred_element_type=F32)
+                picked[g, pl.ds(t * 2 * PAIRS, 2 * PAIRS), :] = rows.astype(BF16)
+
+            @pl.when(g != group)
+            def _():
+                deliver(g, part).start()
+
+            @pl.when(g == group)
+            def _():
+                rows = pl.ds(part * TG * 2 * PAIRS, TG * 2 * PAIRS)
+                halo[1 + group, rows, :] = picked[g, rows, :]
+
+            @pl.when(to_low)
+            def _():
+                edge(g, part, hour - 1, 5).start()
+
+            @pl.when(to_high)
+            def _():
+                edge(g, part, hour + 1, 0).start()
+
+            return 0
+
+        lax.fori_loop(0, GROUPS, finish, 0)
+
+    def out_wait(slot, part):
+        rows = pl.ds(part * TG * 2 * PAIRS, TG * 2 * PAIRS)
         pltpu.make_async_remote_copy(
-            src_ref=picked.at[0],
-            dst_ref=halo.at[slot],
-            send_sem=out_send.at[0],
-            recv_sem=out_recv.at[slot],
+            src_ref=picked.at[0, rows],
+            dst_ref=halo.at[slot, rows],
+            send_sem=out_send.at[0, part],
+            recv_sem=out_recv.at[slot, part],
             device_id=(chan, hour),
             device_id_type=MESH,
         ).wait_recv()
 
-    others(lambda g: out_wait(1 + g))
-
-    @pl.when(hour > 0)
-    def _():
-        out_wait(0)
-
-    @pl.when(hour < HOUR_DEVS - 1)
-    def _():
-        out_wait(5)
-
-    for b in range(4):
-        total = jnp.dot(halo[b], kernel[0, b], preferred_element_type=F32)
-        for d in range(1, 3):
-            total += jnp.dot(halo[b + d], kernel[d, b], preferred_element_type=F32)
-        for t in range(TURNS):
-            for c in range(2):
-                for p in range(0, PAIRS, 8):
-                    at = t * 2 * PAIRS + c * PAIRS + p
-                    merged[pl.ds((t * PAIRS + p) * 8 + b * 2 + c, 8, stride=8), :] = (
-                        total[at : at + 8]
-                    )
-    out[...] = merged[...].astype(BF16)
+    loads[3].wait()
+    for part in range(PARTS):
+        others(lambda g: out_wait(1 + g, part))
+
+        @pl.when(hour > 0)
+        def _():
+            out_wait(0, part)
+
+        @pl.when(hour < HOUR_DEVS - 1)
+        def _():
+            out_wait(5, part)
+
+        rows = pl.ds(part * TG * 2 * PAIRS, TG * 2 * PAIRS)
+        for b in range(4):
+            total = jnp.dot(halo[b, rows, :], kernel[0, b], preferred_element_type=F32)
+            for d in range(1, 3):
+                total += jnp.dot(
+                    halo[b + d, rows, :], kernel[d, b], preferred_element_type=F32
+                )
+            for t in range(TG):
+                for c in range(2):
+                    for p in range(0, PAIRS, 8):
+                        at = t * 2 * PAIRS + c * PAIRS + p
+                        pair = (part * TG + t) * PAIRS + p
+                        merged[pl.ds(pair * 8 + b * 2 + c, 8, stride=8), :] = total[
+                            at : at + 8
+                        ]
+        done = pl.ds(part * TG * PAIRS * 8, TG * PAIRS * 8)
+        out[done, :] = merged[done, :].astype(BF16)
 
     def drain(n, _):
         g, h = n // HOUR_DEVS, n % HOUR_DEVS
@@ -393,11 +427,13 @@
 
     lax.fori_loop(0, NB, drain, 0)
     others(lambda g: hot_copy(g).wait_send())
-    others(lambda g: deliver(g).wait_send())
+    for part in range(PARTS):
+        others(lambda g: deliver(g, part).wait_send())
 
     def drain_hops(s, _):
-        hop(up, s, up_send, up_recv, above).wait_send()
-        hop(down, s, down_send, down_recv, below).wait_send()
+        for part in range(PARTS):
+            hop(up, s, part, up_send, up_recv, above).wait_send()
+            hop(down, s, part, down_send, down_recv, below).wait_send()
         return 0
 
     lax.fori_loop(0, Z - 1, drain_hops, 0)
@@ -405,7 +441,8 @@
     @pl.when(jnp.logical_or(to_low, to_high))
     def _():
         def each(g, _):
-            edge(g, hour, 0).wait_send()
+            for part in range(PARTS):
+                edge(g, part, hour, 0).wait_send()
             return 0
 
         lax.fori_loop(0, GROUPS, each, 0)
@@ -415,13 +452,13 @@
     tiles = spectra.reshape(HOURS_DEV, C_DEV, 2, NB, BAND)
     tiles = tiles.transpose(0, 1, 3, 2, 4).reshape(HOURS_DEV * C_DEV * NB * 2, BAND)
     vmem = pl.BlockSpec(memory_space=pltpu.VMEM)
-    smem = pl.BlockSpec(memory_space=pltpu.SMEM)
+    hbm = pl.BlockSpec(memory_space=pl.ANY)
     rows = TURNS * 2 * PAIRS
     dma = pltpu.SemaphoreType.DMA
     result = pl.pallas_call(
         body,
         out_shape=jax.ShapeDtypeStruct((rows * 4, BAND), BF16),
-        in_specs=[pl.BlockSpec(memory_space=pl.ANY), vmem, smem, smem, vmem, vmem],
+        in_specs=[hbm, hbm, hbm, hbm, vmem, vmem],
         out_specs=vmem,
         scratch_shapes=[
             pltpu.VMEM((HOURS_DEV * C_DEV * NB * 2, BAND), F32),
@@ -435,22 +472,24 @@
             pltpu.VMEM((GROUPS, rows, BAND), BF16),
             pltpu.VMEM((6, rows, BAND), BF16),
             pltpu.VMEM((rows * 4, BAND), F32),
-            dma,
+            pltpu.VMEM((3, 4, BAND, BAND), BF16),
+            pltpu.SMEM((TURNS,), jnp.int32),
+            pltpu.SMEM((TURNS,), jnp.int32),
+            dma((4,)),
             dma((NB,)),
             dma((GROUPS, HOUR_DEVS)),
-            dma((Z,)),
-            dma((Z,)),
-            dma((Z,)),
-            dma((Z,)),
+            dma((Z, PARTS)),
+            dma((Z, PARTS)),
+            dma((Z, PARTS)),
+            dma((Z, PARTS)),
             dma((GROUPS,)),
             dma((GROUPS,)),
-            dma((GROUPS,)),
-            dma((6,)),
-            dma((GROUPS,)),
-            dma,
+            dma((GROUPS, PARTS)),
+            dma((6, PARTS)),
+            dma((GROUPS, PARTS)),
         ],
         compiler_params=pltpu.CompilerParams(
-            collective_id=0, has_side_effects=True, vmem_limit_bytes=48 * 1024 * 1024
+            collective_id=0, has_side_effects=True, vmem_limit_bytes=63 * 1024 * 1024
         ),
     )(
         tiles,

time: 65.9 us -> 54.8 us (0.83); the launches traced: 65.7 us -> 53.8 us
  Pallas kernels: 60 us -> 51.9 us
  local copies, waits for them, and re-layouts: 5.73 us -> 1.83 us
    pallas_call x1, Pallas kernels: 60 us -> 51.9 us  [local(): pl.pallas_call(body, out_shape=jax.ShapeDtypeStruct((rows * 4, BAND), BF1...]
    unnamed x13 -> x1, local copies, waits for them, and re-layouts: 5.73 us -> 1.83 us
where the time goes in v2:
time: 54.8 us; the launch traced here: 53.8 us
  Pallas kernels  51.9 us (95%)
  local copies, waits for them, and re-layouts  1.83 us (3%)
    pallas_call x1, Pallas kernels, local(): pl.pallas_call(body, out_shape=jax.ShapeDtypeStruct((rows * 4, BAND), BF1...  51.9 us
    unnamed x1, local copies, waits for them, and re-layouts  1.83 us

profile of v2, /device:TPU:2, one launch (start us, length us, event | category | flops | bytes accessed | tf_op | source)
XLA Modules:
  0.0 53.8 jit_solution(7495300105052289686)
XLA Ops:
  0.0 51.9 %shard_map.64 = bf16[1024,128]{1,0:T(8,128)(2,1)} custom-call(f32[3072,128]{1,0:T(8,128)} %bitcast.12, bf16[3,4,128,128]{3,2,1,0:T(8,128)(2,1)} %kernel_hbm.1, s32[4]{0:T(128)} %owners_hbm.1, s32[4]{0:T(128)} %order_hbm.1, s32[1,32]{1,0:T(1,128)} %bitcast.14, s32[1,32]{1,0:T(1,128)} %bitcast.15), custom_call_target="tpu_custom_call" | custom-call | tf_op jit(solution)/shard_map/pallas_call | solution.py:458
  51.9 1.8 %copy.10 = bf16[4,32,2,512]{3,2,1,0:T(2,128)(2,1)} copy(bf16[4,32,2,512]{3,2,1,0:T(2,128)(2,1)} %bitcast.13) | data formatting | bytes 524288

commit v3 on v2

--- a/solution.py
+++ b/solution.py
@@ -18,15 +18,17 @@
 ROWS = HOURS_DEV * 16
 TG = 2
 PARTS = TURNS // TG
+FIRST = 32
+PACED = 0
 NB = 32
 BF16 = jnp.bfloat16
 F32 = jnp.float32
 
 
 def body(
-    spectra, kernel_hbm, owners_hbm, order_hbm, source_pick, receiver_pick, out,
+    spectra, kernel_hbm, owners_hbm, order_hbm, source_hbm, receiver_hbm, out,
     raw, staged, recv, up, down, chosen, acc, onehot, picked, halo, merged,
-    kernel, owner_ids, turn_order, load_sem,
+    kernel, owner_ids, turn_order, source_pick, receiver_pick, load_sem,
     a2a_send, a2a_recv, up_send, up_recv, down_send, down_recv,
     hot_send, hot_recv, out_send, out_recv, edge_send,
 ):
@@ -47,6 +49,8 @@
                 (spectra, raw),
                 (owners_hbm, owner_ids),
                 (order_hbm, turn_order),
+                (source_hbm, source_pick),
+                (receiver_hbm, receiver_pick),
                 (kernel_hbm, kernel),
             ]
         )
@@ -72,6 +76,9 @@
     lax.fori_loop(0, NB, greet, 0)
     pl.semaphore_signal(barrier, inc=1, device_id=(above, hour), device_id_type=MESH)
     pl.semaphore_signal(barrier, inc=1, device_id=(below, hour), device_id_type=MESH)
+
+    for load in loads[3:5]:
+        load.wait()
 
     src = source_pick[...]
     rec = receiver_pick[...]
@@ -110,12 +117,15 @@
             device_id_type=MESH,
         )
 
-    def scatter(n, _):
+    def target(n):
         k = n // GROUPS
         g = (group + n) % GROUPS
         step = (k + 1) // 2
         shift = jnp.where(k % 2 == 1, step, 2 * Z - step)
-        h = (hour + 4 * Z - z - shift) % HOUR_DEVS
+        return g, (hour + 4 * Z - z - shift) % HOUR_DEVS
+
+    def scatter(n, _):
+        g, h = target(n)
         band = h * GROUPS + g
         mine = jnp.logical_and(g == group, h == hour)
         for i in range(HOURS_DEV):
@@ -134,7 +144,18 @@
 
         return 0
 
-    lax.fori_loop(0, NB, scatter, 0)
+    def drain(n, _):
+        g, h = target(n)
+
+        @pl.when(jnp.logical_or(g != group, h != hour))
+        def _():
+            a2a(g, h).wait_send()
+
+        return 0
+
+    lax.fori_loop(0, FIRST, scatter, 0)
+    lax.fori_loop(0, PACED, drain, 0)
+    lax.fori_loop(FIRST, NB, scatter, 0)
 
     def hot_copy(g):
         return pltpu.make_async_remote_copy(
@@ -267,32 +288,36 @@
                     acc[g, t0 + t, k, c] = sums[n]
                     n += 1
 
-    def step(s, first):
-        low, high = hour_of(z - s), hour_of(z + 1 + s)
+    def climb(s, part, first=False):
+        if not first:
+            arrived(up, s, part, up_send, up_recv, below)
+        merge(up, s, hour_of(z - s), part * TG, first)
+        hop(up, s, part, up_send, up_recv, above).start()
+
+    def descend(s, part, first=False):
+        if not first:
+            arrived(down, s, part, down_send, down_recv, above)
+        merge(down, s, hour_of(z + 1 + s), part * TG, first)
+        hop(down, s, part, down_send, down_recv, below).start()
+
+    def step(s):
         for part in range(PARTS):
-            if not first:
-                arrived(up, s, part, up_send, up_recv, below)
-            merge(up, s, low, part * TG, first)
-            hop(up, s, part, up_send, up_recv, above).start()
-            if not first:
-                arrived(down, s, part, down_send, down_recv, above)
-            merge(down, s, high, part * TG, first)
-            hop(down, s, part, down_send, down_recv, below).start()
-        return low, high
+            climb(s, part)
+        for part in range(PARTS):
+            descend(s, part)
 
     def early(s, _):
         wait_pieces(hour_of(z - s))
+        for part in range(PARTS):
+            climb(s, part)
         wait_pieces(hour_of(z + 1 + s))
-        step(s, False)
-
-        @pl.when(s == 1)
-        def _():
-            others(lambda g: hot_copy(g).start())
-
+        for part in range(PARTS):
+            descend(s, part)
         return 0
 
     def late(s, _):
-        low, high = step(s, False)
+        step(s)
+        low, high = hour_of(z - s), hour_of(z + 1 + s)
         choose(s, 0, range(TURNS))
         choose(Z - 1 - s, 1, range(TURNS))
 
@@ -304,8 +329,12 @@
         return 0
 
     wait_pieces(hour_of(z))
+    for part in range(PARTS):
+        climb(0, part, True)
     wait_pieces(hour_of(z + 1))
-    step(0, True)
+    for part in range(PARTS):
+        descend(0, part, True)
+    others(lambda g: hot_copy(g).start())
     lax.fori_loop(1, 4, early, 0)
     lax.fori_loop(4, Z - 1, late, 0)
     low, high = hour_of(z + 1), hour_of(z)
@@ -386,7 +415,7 @@
             device_id_type=MESH,
         ).wait_recv()
 
-    loads[3].wait()
+    loads[5].wait()
     for part in range(PARTS):
         others(lambda g: out_wait(1 + g, part))
 
@@ -416,16 +445,7 @@
         done = pl.ds(part * TG * PAIRS * 8, TG * PAIRS * 8)
         out[done, :] = merged[done, :].astype(BF16)
 
-    def drain(n, _):
-        g, h = n // HOUR_DEVS, n % HOUR_DEVS
-
-        @pl.when(jnp.logical_or(g != group, h != hour))
-        def _():
-            a2a(g, h).wait_send()
-
-        return 0
-
-    lax.fori_loop(0, NB, drain, 0)
+    lax.fori_loop(PACED, NB, drain, 0)
     others(lambda g: hot_copy(g).wait_send())
     for part in range(PARTS):
         others(lambda g: deliver(g, part).wait_send())
@@ -452,13 +472,13 @@
     tiles = spectra.reshape(HOURS_DEV, C_DEV, 2, NB, BAND)
     tiles = tiles.transpose(0, 1, 3, 2, 4).reshape(HOURS_DEV * C_DEV * NB * 2, BAND)
     vmem = pl.BlockSpec(memory_space=pltpu.VMEM)
-    hbm = pl.BlockSpec(memory_space=pl.ANY)
+    hbm = pl.BlockSpec(memory_space=pltpu.HBM)
     rows = TURNS * 2 * PAIRS
     dma = pltpu.SemaphoreType.DMA
     result = pl.pallas_call(
         body,
-        out_shape=jax.ShapeDtypeStruct((rows * 4, BAND), BF16),
-        in_specs=[hbm, hbm, hbm, hbm, vmem, vmem],
+        out_shape=pltpu.VMEM((rows * 4, BAND), BF16),
+        in_specs=[hbm] * 6,
         out_specs=vmem,
         scratch_shapes=[
             pltpu.VMEM((HOURS_DEV * C_DEV * NB * 2, BAND), F32),
@@ -475,7 +495,9 @@
             pltpu.VMEM((3, 4, BAND, BAND), BF16),
             pltpu.SMEM((TURNS,), jnp.int32),
             pltpu.SMEM((TURNS,), jnp.int32),
-            dma((4,)),
+            pltpu.VMEM((1, PAIRS), jnp.int32),
+            pltpu.VMEM((1, PAIRS), jnp.int32),
+            dma((6,)),
             dma((NB,)),
             dma((GROUPS, HOUR_DEVS)),
             dma((Z, PARTS)),

time: 54.8 us -> 51.8 us (0.945); the launches traced: 53.8 us -> 51.7 us
  local copies, waits for them, and re-layouts: 1.83 us -> 0.71 us
  Pallas kernels: 51.9 us -> 51 us
    unnamed x1, local copies, waits for them, and re-layouts: 1.83 us -> 0.71 us
    pallas_call x1, Pallas kernels: 51.9 us -> 51 us  [local(): pl.pallas_call(body, out_shape=pltpu.VMEM((rows * 4, BAND), BF16), in_spe...]
where the time goes in v3:
time: 51.8 us; the launch traced here: 51.7 us
  Pallas kernels  51 us (98%)
  local copies, waits for them, and re-layouts  0.71 us (1%)
    pallas_call x1, Pallas kernels, local(): pl.pallas_call(body, out_shape=pltpu.VMEM((rows * 4, BAND), BF16), in_spe...  51 us

profile of v3, /device:TPU:2, one launch (start us, length us, event | category | flops | bytes accessed | tf_op | source)
XLA Modules:
  0.0 51.7 jit_solution(11074135402111249247)
XLA Ops:
  0.0 51.0 %shard_map.64 = bf16[1024,128]{1,0:T(8,128)(2,1)S(1)} custom-call(f32[3072,128]{1,0:T(8,128)} %bitcast.13, bf16[3,4,128,128]{3,2,1,0:T(8,128)(2,1)} %kernel_hbm.1, s32[4]{0:T(128)} %owners_hbm.1, s32[4]{0:T(128)} %order_hbm.1, s32[1,32]{1,0:T(1,128)} %bitcast.14, s32[1,32]{1,0:T(1,128)} %bitcast.15), custom_call_target="tpu_custom_call" | custom-call | tf_op jit(solution)/shard_map/pallas_call | solution.py:478
  51.0 0.7 %copy.10 = bf16[4,32,2,512]{3,2,1,0:T(2,128)(2,1)} copy(bf16[4,32,2,512]{3,2,1,0:T(2,128)(2,1)S(1)} %bitcast.12) | data formatting | bytes 524288

commit v4 on v3

--- a/solution.py
+++ b/solution.py
@@ -18,8 +18,7 @@
 ROWS = HOURS_DEV * 16
 TG = 2
 PARTS = TURNS // TG
-FIRST = 32
-PACED = 0
+FIRST = 24
 NB = 32
 BF16 = jnp.bfloat16
 F32 = jnp.float32
@@ -117,12 +116,24 @@
             device_id_type=MESH,
         )
 
+    def shift_of(q):
+        q = (q + 2 * Z) % Z
+        return q // 4, q % 4
+
+    def hour_of(q):
+        far, along = shift_of(q)
+        return (hour // 4 + far) % 2 * 4 + (hour + along) % 4
+
+    def hour_for(q):
+        far, along = shift_of(q)
+        return (hour // 4 + far) % 2 * 4 + (hour + 4 - along) % 4
+
     def target(n):
         k = n // GROUPS
         g = (group + n) % GROUPS
         step = (k + 1) // 2
         shift = jnp.where(k % 2 == 1, step, 2 * Z - step)
-        return g, (hour + 4 * Z - z - shift) % HOUR_DEVS
+        return g, hour_for(z + shift)
 
     def scatter(n, _):
         g, h = target(n)
@@ -154,8 +165,6 @@
         return 0
 
     lax.fori_loop(0, FIRST, scatter, 0)
-    lax.fori_loop(0, PACED, drain, 0)
-    lax.fori_loop(FIRST, NB, scatter, 0)
 
     def hot_copy(g):
         return pltpu.make_async_remote_copy(
@@ -240,9 +249,6 @@
             device_id_type=MESH,
         ).wait_recv()
 
-    def hour_of(q):
-        return (q + hour + 4 * Z) % HOUR_DEVS
-
     def choose(r, slot, turns):
         q = z - r + 2 * Z
         for t in turns:
@@ -256,37 +262,38 @@
                 chosen[t, slot, rows, :] = value.astype(F32)
 
     def multiply(g, t0, hours):
-        start = tuple(
-            acc[g, t0 + t, k, c] for t in range(2) for k in range(8) for c in range(2)
-        )
-
-        def each(n, sums):
-            slot, i = n // HOURS_DEV, n % HOURS_DEV
-            h = hours[slot]
-            rows = pl.ds(i * 16, 16)
-            b = recv[g, h, rows, :].astype(F32)
-            b0, b1 = b[:8], b[8:]
-            a = [chosen[t0 + t, slot, rows, :] for t in range(2)]
-            new = list(sums)
-            for k in range(8):
-                r0 = pltpu.roll(b0, 8 - k, 0) if k else b0
-                r1 = pltpu.roll(b1, 8 - k, 0) if k else b1
-                for t in range(2):
-                    a0, a1 = a[t][:8], a[t][8:]
-                    at = (t * 8 + k) * 2
-                    new[at] = new[at] + (a0 * r0 + a1 * r1)
-                    new[at + 1] = new[at + 1] + (a1 * r0 - a0 * r1)
-            return tuple(new)
-
-        sums = start
-        for n in range(2 * HOURS_DEV):
-            sums = each(n, sums)
-        n = 0
-        for t in range(2):
-            for k in range(8):
-                for c in range(2):
-                    acc[g, t0 + t, k, c] = sums[n]
-                    n += 1
+        for k0 in range(0, 8, 4):
+            span = range(k0, k0 + 4)
+            sums = [acc[g, t0 + t, k, c] for t in range(2) for k in span for c in range(3)]
+            for slot in range(2):
+                for i in range(HOURS_DEV):
+                    rows = pl.ds(i * 16, 16)
+                    b = recv[g, hours[slot], rows, :].astype(F32)
+                    b0, b1 = b[:8], b[8:]
+                    a = [chosen[t0 + t, slot, rows, :] for t in range(2)]
+                    a = [(x[:8], x[8:], x[:8] + x[8:]) for x in a]
+                    for k in span:
+                        r0 = pltpu.roll(b0, 8 - k, 0) if k else b0
+                        r1 = pltpu.roll(b1, 8 - k, 0) if k else b1
+                        rd = r0 - r1
+                        for t in range(2):
+                            at = (t * 4 + k - k0) * 3
+                            sums[at] = sums[at] + a[t][0] * r0
+                            sums[at + 1] = sums[at + 1] + a[t][1] * r1
+                            sums[at + 2] = sums[at + 2] + a[t][2] * rd
+            n = 0
+            for t in range(2):
+                for k in span:
+                    for c in range(3):
+                        acc[g, t0 + t, k, c] = sums[n]
+                        n += 1
+
+    def table_of(g, t):
+        parts = []
+        for k in range(8):
+            real, imag, cross = (acc[g, t, k, c] for c in range(3))
+            parts += [real + imag, cross - real + imag]
+        return jnp.concatenate(parts, axis=0).astype(BF16)
 
     def climb(s, part, first=False):
         if not first:
@@ -313,6 +320,13 @@
         wait_pieces(hour_of(z + 1 + s))
         for part in range(PARTS):
             descend(s, part)
+        lax.fori_loop(s * 8 - 8, s * 8, drain, 0)
+        return 0
+
+    def drain_hops(s, _):
+        for part in range(PARTS):
+            hop(up, s, part, up_send, up_recv, above).wait_send()
+            hop(down, s, part, down_send, down_recv, below).wait_send()
         return 0
 
     def late(s, _):
@@ -326,6 +340,7 @@
             return 0
 
         lax.fori_loop(0, GROUPS * 2, each, 0)
+        drain_hops(s - 2, 0)
         return 0
 
     wait_pieces(hour_of(z))
@@ -334,8 +349,12 @@
     wait_pieces(hour_of(z + 1))
     for part in range(PARTS):
         descend(0, part, True)
+    lax.fori_loop(FIRST, NB, scatter, 0)
     others(lambda g: hot_copy(g).start())
     lax.fori_loop(1, 4, early, 0)
+    lax.fori_loop(NB * 3 // 4, NB, drain, 0)
+    others(lambda g: hot_copy(g).wait_send())
+    lax.fori_loop(0, 2, drain_hops, 0)
     lax.fori_loop(4, Z - 1, late, 0)
     low, high = hour_of(z + 1), hour_of(z)
     others(lambda g: hot_wait(g).wait_recv())
@@ -376,12 +395,18 @@
             g = (group + 1 + n) % GROUPS
             for t in turns[::2]:
                 multiply(g, t, (low, high))
-            for t in turns:
-                table = jnp.concatenate(
-                    [acc[g, t, k, c] for k in range(8) for c in range(2)], axis=0
-                ).astype(BF16)
-                rows = jnp.dot(onehot[g], table, preferred_element_type=F32)
-                picked[g, pl.ds(t * 2 * PAIRS, 2 * PAIRS), :] = rows.astype(BF16)
+            table = jnp.concatenate(
+                [
+                    table_of(g, t)
+                    for t in turns
+                ],
+                axis=1,
+            )
+            rows = jnp.dot(onehot[g], table, preferred_element_type=F32).astype(BF16)
+            for n2, t in enumerate(turns):
+                picked[g, pl.ds(t * 2 * PAIRS, 2 * PAIRS), :] = rows[
+                    :, n2 * BAND : (n2 + 1) * BAND
+                ]
 
             @pl.when(g != group)
             def _():
@@ -445,18 +470,10 @@
         done = pl.ds(part * TG * PAIRS * 8, TG * PAIRS * 8)
         out[done, :] = merged[done, :].astype(BF16)
 
-    lax.fori_loop(PACED, NB, drain, 0)
-    others(lambda g: hot_copy(g).wait_send())
     for part in range(PARTS):
         others(lambda g: deliver(g, part).wait_send())
 
-    def drain_hops(s, _):
-        for part in range(PARTS):
-            hop(up, s, part, up_send, up_recv, above).wait_send()
-            hop(down, s, part, down_send, down_recv, below).wait_send()
-        return 0
-
-    lax.fori_loop(0, Z - 1, drain_hops, 0)
+    lax.fori_loop(5, Z - 1, drain_hops, 0)
 
     @pl.when(jnp.logical_or(to_low, to_high))
     def _():
@@ -487,7 +504,7 @@
             pltpu.VMEM((Z, TURNS, ROWS, BAND), BF16),
             pltpu.VMEM((Z, TURNS, ROWS, BAND), BF16),
             pltpu.VMEM((TURNS, 2, ROWS, BAND), F32),
-            pltpu.VMEM((GROUPS, TURNS, 8, 2, 8, BAND), F32),
+            pltpu.VMEM((GROUPS, TURNS, 8, 3, 8, BAND), F32),
             pltpu.VMEM((GROUPS, 2 * PAIRS, BAND), BF16),
             pltpu.VMEM((GROUPS, rows, BAND), BF16),
             pltpu.VMEM((6, rows, BAND), BF16),

time: 51.8 us -> 50.1 us (0.967)
  Pallas kernels: 51 us -> 49.1 us
    pallas_call x1, Pallas kernels: 51 us -> 49.1 us  [local(): pl.pallas_call(body, out_shape=pltpu.VMEM((rows * 4, BAND), BF16), in_spe...]
where the time goes in v4:
time: 50.1 us; the launch traced here: 49.8 us
  Pallas kernels  49.1 us (98%)
  local copies, waits for them, and re-layouts  0.71 us (1%)
    pallas_call x1, Pallas kernels, local(): pl.pallas_call(body, out_shape=pltpu.VMEM((rows * 4, BAND), BF16), in_spe...  49.1 us

profile of v4, /device:TPU:2, one launch (start us, length us, event | category | flops | bytes accessed | tf_op | source)
XLA Modules:
  0.0 49.8 jit_solution(8014670006980767400)
XLA Ops:
  0.0 49.1 %shard_map.64 = bf16[1024,128]{1,0:T(8,128)(2,1)S(1)} custom-call(f32[3072,128]{1,0:T(8,128)} %bitcast.13, bf16[3,4,128,128]{3,2,1,0:T(8,128)(2,1)} %kernel_hbm.1, s32[4]{0:T(128)} %owners_hbm.1, s32[4]{0:T(128)} %order_hbm.1, s32[1,32]{1,0:T(1,128)} %bitcast.14, s32[1,32]{1,0:T(1,128)} %bitcast.15), custom_call_target="tpu_custom_call" | custom-call | tf_op jit(solution)/shard_map/pallas_call | solution.py:495
  49.1 0.7 %copy.10 = bf16[4,32,2,512]{3,2,1,0:T(2,128)(2,1)} copy(bf16[4,32,2,512]{3,2,1,0:T(2,128)(2,1)S(1)} %bitcast.12) | data formatting | bytes 524288

commit v5 on v4

--- a/solution.py
+++ b/solution.py
@@ -20,6 +20,7 @@
 PARTS = TURNS // TG
 FIRST = 24
 NB = 32
+TILE_ROWS = HOURS_DEV * C_DEV * NB * 2
 BF16 = jnp.bfloat16
 F32 = jnp.float32
 
@@ -45,7 +46,7 @@
         pltpu.make_async_copy(a, b, load_sem.at[n])
         for n, (a, b) in enumerate(
             [
-                (spectra, raw),
+                (spectra, raw.at[pl.ds(0, TILE_ROWS)]),
                 (owners_hbm, owner_ids),
                 (order_hbm, turn_order),
                 (source_hbm, source_pick),
@@ -487,7 +488,7 @@
 
 def local(spectra, smooth_kernel, owner_ids, turn_order, source_pick, receiver_pick):
     tiles = spectra.reshape(HOURS_DEV, C_DEV, 2, NB, BAND)
-    tiles = tiles.transpose(0, 1, 3, 2, 4).reshape(HOURS_DEV * C_DEV * NB * 2, BAND)
+    tiles = tiles.transpose(0, 1, 3, 2, 4).reshape(TILE_ROWS, BAND)
     vmem = pl.BlockSpec(memory_space=pltpu.VMEM)
     hbm = pl.BlockSpec(memory_space=pltpu.HBM)
     rows = TURNS * 2 * PAIRS
@@ -498,7 +499,7 @@
         in_specs=[hbm] * 6,
         out_specs=vmem,
         scratch_shapes=[
-            pltpu.VMEM((HOURS_DEV * C_DEV * NB * 2, BAND), F32),
+            pltpu.VMEM((TILE_ROWS + 64, BAND), F32),
             pltpu.VMEM((NB, ROWS, BAND), BF16),
             pltpu.VMEM((GROUPS, HOUR_DEVS, ROWS, BAND), BF16),
             pltpu.VMEM((Z, TURNS, ROWS, BAND), BF16),
@@ -508,7 +509,7 @@
             pltpu.VMEM((GROUPS, 2 * PAIRS, BAND), BF16),
             pltpu.VMEM((GROUPS, rows, BAND), BF16),
             pltpu.VMEM((6, rows, BAND), BF16),
-            pltpu.VMEM((rows * 4, BAND), F32),
+            pltpu.VMEM((rows * 4 + 64, BAND), F32),
             pltpu.VMEM((3, 4, BAND, BAND), BF16),
             pltpu.SMEM((TURNS,), jnp.int32),
             pltpu.SMEM((TURNS,), jnp.int32),

time: 50.1 us -> 50.1 us (level)
  no operation moved by 1% of the time
where the time goes in v5:
time: 50.1 us; the launch traced here: 49.8 us
  Pallas kernels  49.1 us (98%)
  local copies, waits for them, and re-layouts  0.71 us (1%)
    pallas_call x1, Pallas kernels, local(): pl.pallas_call(body, out_shape=pltpu.VMEM((rows * 4, BAND), BF16), in_spe...  49.1 us

profile of v5, /device:TPU:2, one launch (start us, length us, event | category | flops | bytes accessed | tf_op | source)
XLA Modules:
  0.0 49.8 jit_solution(13399955761091327541)
XLA Ops:
  0.0 49.1 %shard_map.64 = bf16[1024,128]{1,0:T(8,128)(2,1)S(1)} custom-call(f32[3072,128]{1,0:T(8,128)} %bitcast.13, bf16[3,4,128,128]{3,2,1,0:T(8,128)(2,1)} %kernel_hbm.1, s32[4]{0:T(128)} %owners_hbm.1, s32[4]{0:T(128)} %order_hbm.1, s32[1,32]{1,0:T(1,128)} %bitcast.14, s32[1,32]{1,0:T(1,128)} %bitcast.15), custom_call_target="tpu_custom_call" | custom-call | tf_op jit(solution)/shard_map/pallas_call | solution.py:496
  49.1 0.7 %copy.10 = bf16[4,32,2,512]{3,2,1,0:T(2,128)(2,1)} copy(bf16[4,32,2,512]{3,2,1,0:T(2,128)(2,1)S(1)} %bitcast.12) | data formatting | bytes 524288

commit v6 on v5

--- a/solution.py
+++ b/solution.py
@@ -441,6 +441,8 @@
             device_id_type=MESH,
         ).wait_recv()
 
+    lax.fori_loop(5, Z - 1, drain_hops, 0)
+
     loads[5].wait()
     for part in range(PARTS):
         others(lambda g: out_wait(1 + g, part))
@@ -474,7 +476,6 @@
     for part in range(PARTS):
         others(lambda g: deliver(g, part).wait_send())
 
-    lax.fori_loop(5, Z - 1, drain_hops, 0)
 
     @pl.when(jnp.logical_or(to_low, to_high))
     def _():

time: 50.1 us -> 50.1 us (level)
  no operation moved by 1% of the time
where the time goes in v6:
time: 50.1 us; the launch traced here: 49.8 us
  Pallas kernels  49.1 us (98%)
  local copies, waits for them, and re-layouts  0.71 us (1%)
    pallas_call x1, Pallas kernels, local(): pl.pallas_call(body, out_shape=pltpu.VMEM((rows * 4, BAND), BF16), in_spe...  49.1 us

profile of v6, /device:TPU:2, one launch (start us, length us, event | category | flops | bytes accessed | tf_op | source)
XLA Modules:
  0.0 49.8 jit_solution(5168296957040428482)
XLA Ops:
  0.0 49.1 %shard_map.64 = bf16[1024,128]{1,0:T(8,128)(2,1)S(1)} custom-call(f32[3072,128]{1,0:T(8,128)} %bitcast.13, bf16[3,4,128,128]{3,2,1,0:T(8,128)(2,1)} %kernel_hbm.1, s32[4]{0:T(128)} %owners_hbm.1, s32[4]{0:T(128)} %order_hbm.1, s32[1,32]{1,0:T(1,128)} %bitcast.14, s32[1,32]{1,0:T(1,128)} %bitcast.15), custom_call_target="tpu_custom_call" | custom-call | tf_op jit(solution)/shard_map/pallas_call | solution.py:497
  49.1 0.7 %copy.10 = bf16[4,32,2,512]{3,2,1,0:T(2,128)(2,1)} copy(bf16[4,32,2,512]{3,2,1,0:T(2,128)(2,1)S(1)} %bitcast.12) | data formatting | bytes 524288
